TPU v7x, 32 devices: a whole 2x2x4 slice. The times are simulated.
32 devices in a mesh: groups: 2 (over y), row: 8 (over z, x), col: 2 (over core).
Axes of the slice: x: 2, y: 2, z: 4, core: 2. Of those that a mesh axis runs over, the one named last changes fastest.
Arguments:
- states: bfloat16 [2, 32, 2, 8192], P(None, ('groups', 'row'), 'col'), parts along dimension 1, may hold values from -60 to 60
- norm_gain: float32 [2, 8192], P('col'), may hold values from 0.1 to 1.9
- w_query: bfloat16 [2, 2, 6144, 8192], P('col', None, 'row'), may hold values from -0.046875 to 0.046875
- w_key: bfloat16 [2, 2, 384, 8192], P('col', None, 'row'), may hold values from -0.046875 to 0.046875
- w_value: bfloat16 [2, 2, 384, 8192], P('col', None, 'row'), may hold values from -0.046875 to 0.046875
- w_out: bfloat16 [2, 2, 8192, 6144], P('col', None, 'row'), may hold values from -0.3125 to 0.3125
- key_cache: bfloat16 [32, 256, 6, 128], P(('groups', 'row'), None, 'col'), parts along dimension 0, may hold values from -260 to 260
- value_cache: bfloat16 [32, 256, 6, 128], P(('groups', 'row'), None, 'col'), parts along dimension 0, may hold values from -6 to 6
- cache_len: int32 [32], P(('groups', 'row')), parts along dimension 0, may hold values from 1 to 256, as said below
- slot_row: int32 [32], P('groups'), parts along dimension 0, may hold values from 0 to 15, each once
- exit_layer: int32 [2, 32], P(None, 'groups'), parts along dimension 1, may hold values from 0 to 125
Outputs:
- mixed: bfloat16 [2, 32, 2, 8192], P(None, 'groups', 'col', 'row'), parts along dimension 1
There are 2 independent parts, one for each index of `groups`. A program takes and returns all parts, laid end to end along the dimension named above; an argument that names none is the same for every part. Nothing has to cross between parts.
Inputs may be any that keep to these rules, and one draw needn't show every extreme that they name: `cache_len`: some cache row is full in every draw. `slot_row`: each batch row appears once.
All inputs are finite; a program needn't handle non-finite values.
Results may differ from a plain program's by a relative error of at most 0.012.
The roundings to bfloat16 on the way count: a program that leaves them out, or rounds other values in their place, can miss the bound.
Values may be sent and summed in bfloat16 or wider, within the bound.
A program may use at most 128 MiB of HBM per device.

v0:
```python
import jax
import jax.numpy as jnp
from jax import lax
from jax.sharding import PartitionSpec as P

LAYER_AT = 63


epsilon = 1e-05


def on_device(
    states,
    norm_gain,
    w_query,
    w_key,
    w_value,
    w_out,
    key_cache,
    value_cache,
    cache_len,
    slot_row,
    exit_layer,
):
    row_count = lax.axis_size("row")
    row_index = lax.axis_index("row")
    own_rows = key_cache.shape[0]
    half_width = states.shape[3]
    model_width = half_width * w_query.shape[1]
    kv_local = key_cache.shape[2]
    head_size = key_cache.shape[3]
    group_size = w_query.shape[2] * row_count // (kv_local * head_size)
    piece_width = w_out.shape[2]
    scale_factor = head_size ** (-0.5)
    cache_slots = key_cache.shape[1]
    step_total = states.shape[0]
    valid_mask = jnp.arange(cache_slots)[None, :] < cache_len[:, None]
    own_slots = lax.dynamic_slice_in_dim(slot_row, row_index * own_rows, own_rows)
    gain_local = norm_gain[None]
    block_size = 1
    new_keys = []
    new_values = []
    results = []
    for first_step in range(0, step_total, block_size):
        block = states[first_step : first_step + block_size]
        gathered = lax.all_gather(block, "row", axis=1, tiled=True)
        widened = gathered.astype(jnp.float32)
        squares = jnp.sum(jnp.square(widened), axis=3)
        totals = lax.psum(squares, "col")
        scaling = lax.rsqrt(totals / model_width + epsilon)
        normed = (widened * scaling[..., None] * gain_local).astype(jnp.bfloat16)[:, :, 0, :]
        query_part = jnp.einsum(
            "srd,hcd->srhc", normed, w_query[0], preferred_element_type=jnp.float32
        )
        key_part = jnp.einsum("srd,hcd->srhc", normed, w_key[0], preferred_element_type=jnp.float32)
        value_part = jnp.einsum(
            "srd,hcd->srhc", normed, w_value[0], preferred_element_type=jnp.float32
        )
        query_sum, key_sum, value_sum = (
            lax.psum_scatter(query_part, "col", scatter_dimension=2, tiled=True),
            lax.psum_scatter(key_part, "col", scatter_dimension=2, tiled=True),
            lax.psum_scatter(value_part, "col", scatter_dimension=2, tiled=True),
        )
        query_sorted = jnp.take(query_sum.astype(jnp.bfloat16), slot_row, axis=1)
        key_sorted = jnp.take(key_sum.astype(jnp.bfloat16), slot_row, axis=1)
        value_sorted = jnp.take(value_sum.astype(jnp.bfloat16), slot_row, axis=1)
        query_own, key_own, value_own = (
            lax.all_to_all(query_sorted, "row", split_axis=1, concat_axis=3, tiled=True),
            lax.all_to_all(key_sorted, "row", split_axis=1, concat_axis=3, tiled=True),
            lax.all_to_all(value_sorted, "row", split_axis=1, concat_axis=3, tiled=True),
        )
        queries = query_own[0].reshape(own_rows, kv_local, group_size, head_size)
        new_keys.append(key_own[0].reshape(own_rows, kv_local, head_size))
        new_values.append(value_own[0].reshape(own_rows, kv_local, head_size))
        cache_scores = (
            jnp.einsum("bghd,blgd->bghl", queries, key_cache, preferred_element_type=jnp.float32)
            * scale_factor
        )
        cache_scores = jnp.where(valid_mask[:, None, None, :], cache_scores, -jnp.inf)
        fresh_scores = (
            jnp.stack(
                [
                    jnp.einsum(
                        "bghd,bgd->bgh", queries, earlier, preferred_element_type=jnp.float32
                    )
                    for earlier in new_keys
                ],
                axis=-1,
            )
            * scale_factor
        )
        largest = jnp.maximum(jnp.max(cache_scores, axis=-1), jnp.max(fresh_scores, axis=-1))
        cache_exps = jnp.exp(cache_scores - largest[..., None])
        fresh_exps = jnp.exp(fresh_scores - largest[..., None])
        denominator = jnp.sum(cache_exps, axis=-1) + jnp.sum(fresh_exps, axis=-1)
        weights_cache = (cache_exps / denominator[..., None]).astype(jnp.bfloat16)
        weights_fresh = (fresh_exps / denominator[..., None]).astype(jnp.bfloat16)
        attended = jnp.einsum(
            "bghl,blgd->bghd", weights_cache, value_cache, preferred_element_type=jnp.float32
        )
        attended = attended + jnp.einsum(
            "bght,btgd->bghd",
            weights_fresh,
            jnp.stack(new_values, axis=1),
            preferred_element_type=jnp.float32,
        )
        active = jnp.take(exit_layer[first_step], own_slots) > LAYER_AT
        attended = (
            jnp.where(active[:, None, None, None], attended, 0.0)
            .astype(jnp.bfloat16)
            .reshape(own_rows, -1)
        )
        attended_block = [attended]
        attended_all = jnp.stack(attended_block)
        projection_terms = jnp.einsum(
            "srf,hcf->srhc",
            lax.all_gather(attended_all, "row", axis=1, tiled=True),
            w_out[0],
            preferred_element_type=jnp.float32,
        )
        projected = lax.psum_scatter(projection_terms, "col", scatter_dimension=2, tiled=True)
        reordered = jnp.zeros_like(projected).at[:, slot_row].set(projected)
        residual = lax.dynamic_slice_in_dim(
            gathered, row_index * piece_width, piece_width, 3
        ).astype(jnp.float32)
        results.append((residual + reordered).astype(jnp.bfloat16))
    return jnp.concatenate(results, axis=0)


def solution(mesh):
    return jax.shard_map(
        on_device,
        mesh=mesh,
        in_specs=(
            P(None, ("groups", "row"), "col", None),
            P("col", None),
            P("col", None, "row", None),
            P("col", None, "row", None),
            P("col", None, "row", None),
            P("col", None, "row", None),
            P(("groups", "row"), None, "col", None),
            P(("groups", "row"), None, "col", None),
            P(("groups", "row")),
            P("groups"),
            P(None, "groups"),
        ),
        out_specs=P(None, "groups", "col", "row"),
        check_vma=False,
    )
```

profile of v0, /device:TPU:0, one launch (start us, length us, event | category | flops | bytes accessed | tf_op | source)
XLA Modules:
  0.0 284.1 jit_solution(4186358202019422552)
XLA Ops:
  6.5 0.9 fusion.90
  7.5 33.0 %all_gather.12 = bf16[1,16,1,8192]{3,2,0,1:T(2,128)(2,1)S(1)} all-gather(bf16[1,2,1,8192]{3,2,0,1:T(2,128)(2,1)S(1)} %copy.147), channel_id=1, replica_groups=mesh['groups'=2,'row'=8,'col'=2] {'row'}, dimensions={1}, use_global_device_ids=true | all-gather | bytes 294912 | tf_op jit(solution)/shard_map/all_gather | solution.py:46
  41.0 31.3 %all_gather.14 = bf16[1,16,1,8192]{3,2,0,1:T(2,128)(2,1)S(1)} all-gather(bf16[1,2,1,8192]{3,2,0,1:T(2,128)(2,1)S(1)} %copy.148), channel_id=1, replica_groups=mesh['groups'=2,'row'=8,'col'=2] {'row'}, dimensions={1}, use_global_device_ids=true | all-gather | bytes 294912 | tf_op jit(solution)/shard_map/all_gather | solution.py:46
  72.7 2.5 all-reduce
  75.2 2.3 fusion.40
  77.5 2.9 %fusion.37 = f32[1,16,2,48]{3,1,2,0:T(8,128)} fusion(bf16[1,2,48,8192]{3,2,1,0:T(8,128)(2,1)} %param.20, bf16[1,16,1,8192]{3,1,2,0:T(8,128)(2,1)S(1)} %get-tuple-element.13, f32[16]{0:T(128)S(1)} %rsqrt_bitcast_fusion, f32[8192]{0:T(1024)} %bitcast.210), kind=kOutput, calls=%fused_computation.41 | convolution fusion | flops 25690112 | bytes 1873984 | tf_op jit(solution)/shard_map/srd,hcd->srhc/dot_general | solution.py:55
  80.5 2.3 fusion.43
  82.9 2.9 %fusion.34 = f32[1,16,2,48]{3,1,2,0:T(8,128)} fusion(bf16[1,2,48,8192]{3,2,1,0:T(8,128)(2,1)} %param.20, bf16[1,16,1,8192]{3,1,2,0:T(8,128)(2,1)S(1)} %get-tuple-element.11, f32[8192]{0:T(1024)} %bitcast.212, f32[16]{0:T(128)S(1)} %rsqrt_bitcast_fusion.1), kind=kOutput, calls=%fused_computation.40 | convolution fusion | flops 25690112 | bytes 1873984 | tf_op jit(solution)/shard_map/srd,hcd->srhc/dot_general | solution.py:55
  85.9 12.2 %fusion.22 = f32[1,16,2,768]{3,1,2,0:T(8,128)} fusion(bf16[1,2,768,8192]{3,2,1,0:T(8,128)(2,1)} %param.19, bf16[1,16,1,8192]{3,1,2,0:T(8,128)(2,1)S(1)} %get-tuple-element.11, f32[8192]{0:T(1024)} %bitcast.213, f32[16]{0:T(128)S(1)} %rsqrt_bitcast_fusion.1), kind=kOutput, calls=%fused_computation.28 | convolution fusion | flops 403177472 | bytes 25559104 | tf_op jit(solution)/shard_map/srd,hcd->srhc/dot_general | solution.py:52
  98.2 12.2 %fusion.25 = f32[1,16,2,768]{3,1,2,0:T(8,128)} fusion(bf16[1,2,768,8192]{3,2,1,0:T(8,128)(2,1)} %param.19, bf16[1,16,1,8192]{3,1,2,0:T(8,128)(2,1)S(1)} %get-tuple-element.13, f32[16]{0:T(128)S(1)} %rsqrt_bitcast_fusion, f32[8192]{0:T(1024)S(1)} %bitcast.214), kind=kOutput, calls=%fused_computation.29 | convolution fusion | flops 403177472 | bytes 25559104 | tf_op jit(solution)/shard_map/srd,hcd->srhc/dot_general | solution.py:52
  110.6 0.6 gather_fusion
  111.2 0.6 gather_fusion.4
  111.9 0.7 convert_bitcast_fusion.4
  113.2 0.7 convert_bitcast_fusion.3
  114.5 0.7 convert_bitcast_fusion.2
  115.8 2.6 reduce-scatter.11.cloned.1.call-done
  118.4 0.7 convert_bitcast_fusion.5
  119.8 0.6 copy.114
  120.4 5.7 %all-to-all-start.2 = ((bf16[1,16,1,48]{3,2,0,1:T(2,128)(2,1)}), bf16[1,16,1,48]{3,2,0,1:T(2,128)(2,1)S(1)}, u32[]{:S(2)}, u32[]{:S(2)}) async-start(bf16[1,16,1,48]{3,2,0,1:T(2,128)(2,1)} %copy.114), calls=%async_computation.5 | async-start | bytes 16384 | tf_op jit(solution)/shard_map/all_to_all | solution.py:70
  126.2 0.6 copy.122
  126.8 0.6 copy.112
  127.4 0.6 copy.128
  128.0 4.6 %all-to-all-done.2 = bf16[1,16,1,48]{3,2,0,1:T(2,128)(2,1)S(1)} async-done(((bf16[1,16,1,48]{3,2,0,1:T(2,128)(2,1)}), bf16[1,16,1,48]{3,2,0,1:T(2,128)(2,1)S(1)}, u32[]{:S(2)}, u32[]{:S(2)}) %all-to-all-start.2) | async-done | bytes 1568 | tf_op jit(solution)/shard_map/all_to_all | solution.py:70
  132.6 3.3 %all-to-all-start.4 = ((bf16[1,16,1,48]{3,2,0,1:T(2,128)(2,1)}), bf16[1,16,1,48]{3,2,0,1:T(2,128)(2,1)S(1)}, u32[]{:S(2)}, u32[]{:S(2)}) async-start(bf16[1,16,1,48]{3,2,0,1:T(2,128)(2,1)} %copy.122), calls=%async_computation.10 | async-start | bytes 16384 | tf_op jit(solution)/shard_map/all_to_all | solution.py:69
  136.0 0.8 convert_bitcast_fusion.1
  136.8 5.6 %all-to-all-done.4 = bf16[1,16,1,48]{3,2,0,1:T(2,128)(2,1)S(1)} async-done(((bf16[1,16,1,48]{3,2,0,1:T(2,128)(2,1)}), bf16[1,16,1,48]{3,2,0,1:T(2,128)(2,1)S(1)}, u32[]{:S(2)}, u32[]{:S(2)}) %all-to-all-start.4) | async-done | bytes 1568 | tf_op jit(solution)/shard_map/all_to_all | solution.py:69
  142.4 3.3 %all-to-all-start.1 = ((bf16[1,16,1,48]{3,2,0,1:T(2,128)(2,1)}), bf16[1,16,1,48]{3,2,0,1:T(2,128)(2,1)S(1)}, u32[]{:S(2)}, u32[]{:S(2)}) async-start(bf16[1,16,1,48]{3,2,0,1:T(2,128)(2,1)} %copy.112), calls=%async_computation.3 | async-start | bytes 16384 | tf_op jit(solution)/shard_map/all_to_all | solution.py:69
  145.8 0.8 convert_bitcast_fusion
  147.8 4.4 %all-to-all-done.1 = bf16[1,16,1,48]{3,2,0,1:T(2,128)(2,1)S(1)} async-done(((bf16[1,16,1,48]{3,2,0,1:T(2,128)(2,1)}), bf16[1,16,1,48]{3,2,0,1:T(2,128)(2,1)S(1)}, u32[]{:S(2)}, u32[]{:S(2)}) %all-to-all-start.1) | async-done | bytes 1568 | tf_op jit(solution)/shard_map/all_to_all | solution.py:69
  152.2 3.3 %all-to-all-start.5 = ((bf16[1,16,1,48]{3,2,0,1:T(2,128)(2,1)}), bf16[1,16,1,48]{3,2,0,1:T(2,128)(2,1)S(1)}, u32[]{:S(2)}, u32[]{:S(2)}) async-start(bf16[1,16,1,48]{3,2,0,1:T(2,128)(2,1)} %copy.128), calls=%async_computation.12 | async-start | bytes 16384 | tf_op jit(solution)/shard_map/all_to_all | solution.py:70
  155.7 0.6 broadcast.241
  156.2 0.8 reduce.6
  157.1 0.6 reshape.349
  157.7 4.3 %all-to-all-done.5 = bf16[1,16,1,48]{3,2,0,1:T(2,128)(2,1)S(1)} async-done(((bf16[1,16,1,48]{3,2,0,1:T(2,128)(2,1)}), bf16[1,16,1,48]{3,2,0,1:T(2,128)(2,1)S(1)}, u32[]{:S(2)}, u32[]{:S(2)}) %all-to-all-start.5) | async-done | bytes 1568 | tf_op jit(solution)/shard_map/all_to_all | solution.py:70
  162.0 3.3 %all-to-all-start.3 = ((bf16[8,2,768]{2,1,0:T(2,128)(2,1)}), bf16[8,2,768]{2,1,0:T(2,128)(2,1)S(1)}, u32[]{:S(2)}, u32[]{:S(2)}) async-start(bf16[8,2,768]{2,1,0:T(2,128)(2,1)} %reshape.349), calls=%async_computation.8 | async-start | bytes 49152 | tf_op jit(solution)/shard_map/all_to_all | solution.py:68
  165.9 0.8 reduce.7
  166.7 0.6 reshape.351
  167.3 4.6 %all-to-all-done.3 = bf16[8,2,768]{2,1,0:T(2,128)(2,1)S(1)} async-done(((bf16[8,2,768]{2,1,0:T(2,128)(2,1)}), bf16[8,2,768]{2,1,0:T(2,128)(2,1)S(1)}, u32[]{:S(2)}, u32[]{:S(2)}) %all-to-all-start.3) | async-done | bytes 24608 | tf_op jit(solution)/shard_map/all_to_all | solution.py:68
  171.9 3.3 %all-to-all-start = ((bf16[8,2,768]{2,1,0:T(2,128)(2,1)}), bf16[8,2,768]{2,1,0:T(2,128)(2,1)S(1)}, u32[]{:S(2)}, u32[]{:S(2)}) async-start(bf16[8,2,768]{2,1,0:T(2,128)(2,1)} %reshape.351), calls=%async_computation.1 | async-start | bytes 49152 | tf_op jit(solution)/shard_map/all_to_all | solution.py:68
  175.7 6.1 %all-to-all-done = bf16[8,2,768]{2,1,0:T(2,128)(2,1)S(1)} async-done(((bf16[8,2,768]{2,1,0:T(2,128)(2,1)}), bf16[8,2,768]{2,1,0:T(2,128)(2,1)S(1)}, u32[]{:S(2)}, u32[]{:S(2)}) %all-to-all-start) | async-done | bytes 24608 | tf_op jit(solution)/shard_map/all_to_all | solution.py:68
  183.8 31.0 %all_gather.15 = bf16[1,16,6144]{2,0,1:T(2,128)(2,1)S(1)} all-gather(bf16[1,2,6144]{2,0,1:T(2,128)(2,1)S(1)} %stack_reshape.9), channel_id=1, replica_groups=mesh['groups'=2,'row'=8,'col'=2] {'row'}, dimensions={1}, use_global_device_ids=true | all-gather | bytes 221184 | tf_op jit(solution)/shard_map/all_gather | solution.py:117
  214.8 12.2 %fusion.19 = f32[1,16,2,1024]{3,1,2,0:T(8,128)} fusion(bf16[1,2,1024,6144]{3,2,1,0:T(8,128)(2,1)} %param.22, bf16[1,16,6144]{2,0,1:T(2,128)(2,1)S(1)} %all_gather.15), kind=kOutput, calls=%fused_computation.27 | convolution fusion | flops 402653184 | bytes 25493504 | tf_op jit(solution)/shard_map/srf,hcf->srhc/dot_general | solution.py:115
  227.5 31.1 %all_gather.13 = bf16[1,16,6144]{2,0,1:T(2,128)(2,1)S(1)} all-gather(bf16[1,2,6144]{2,0,1:T(2,128)(2,1)S(1)} %stack_reshape.8), channel_id=1, replica_groups=mesh['groups'=2,'row'=8,'col'=2] {'row'}, dimensions={1}, use_global_device_ids=true | all-gather | bytes 221184 | tf_op jit(solution)/shard_map/all_gather | solution.py:117
  258.6 12.2 %fusion.16 = f32[1,16,2,1024]{3,1,2,0:T(8,128)} fusion(bf16[1,2,1024,6144]{3,2,1,0:T(8,128)(2,1)} %param.22, bf16[1,16,6144]{2,0,1:T(2,128)(2,1)S(1)} %all_gather.13), kind=kOutput, calls=%fused_computation.26 | convolution fusion | flops 402653184 | bytes 25493504 | tf_op jit(solution)/shard_map/srf,hcf->srhc/dot_general | solution.py:115
  270.8 1.0 scatter_custom_fusion.1
  271.8 3.8 %reduce-scatter.15.cloned.1.call-done = f32[1,16,1,1024]{3,1,2,0:T(8,128)} async-done(((f32[1,16,2,1024]{3,1,2,0:T(8,128)}), f32[1,16,1,1024]{3,1,2,0:T(8,128)}) %reduce-scatter.15.cloned.1.call-update) | async-done | bytes 65552 | tf_op jit(solution)/shard_map/reduce_scatter | solution.py:121
  275.6 1.0 scatter_custom_fusion
  276.6 0.6 pad_maximum_fusion
  (107 shorter events, 8.7 us)
Async XLA Ops:
  6.5 68.7 %copy-start = (bf16[1,2,48,8192]{3,2,1,0:T(8,128)(2,1)S(1)}, bf16[1,2,48,8192]{3,2,1,0:T(8,128)(2,1)}, u32[]{:S(2)}) copy-start(bf16[1,2,48,8192]{3,2,1,0:T(8,128)(2,1)} %param.21) | copy-start | bytes 4718596
  6.5 105.4 %reduce-scatter.13.cloned.1.call-start = ((), (), s32[]{:S(2)}) async-start(), calls=%async_computation.16 | async-start | bytes 24576 | tf_op jit(solution)/shard_map/reduce_scatter | solution.py:62
  77.5 35.8 %reduce-scatter.19.cloned.1.call-start = ((), (), s32[]{:S(2)}) async-start(), calls=%async_computation.19 | async-start | bytes 24576 | tf_op jit(solution)/shard_map/reduce_scatter | solution.py:61
  80.5 17.7 %copy-start.1 = (f32[1,8192]{1,0:T(1,128)S(1)}, f32[1,8192]{1,0:T(1,128)}, u32[]{:S(2)}) copy-start(f32[1,8192]{1,0:T(1,128)} %param.18) | copy-start | bytes 98308
  80.5 34.1 %reduce-scatter.21.cloned.1.call-start = ((), (), s32[]{:S(2)}) async-start(), calls=%async_computation.20 | async-start | bytes 24576 | tf_op jit(solution)/shard_map/reduce_scatter | solution.py:62
  82.8 35.6 %reduce-scatter.11.cloned.1.call-start = ((), (), s32[]{:S(2)}) async-start(), calls=%async_computation.15 | async-start | bytes 24576 | tf_op jit(solution)/shard_map/reduce_scatter | solution.py:61
  85.8 50.2 %reduce-scatter.9.cloned.1.call-start = ((), (), s32[]{:S(2)}) async-start(), calls=%async_computation.14 | async-start | bytes 147456 | tf_op jit(solution)/shard_map/reduce_scatter | solution.py:60
  98.1 12.4 %copy-start.4 = (s32[16]{0:T(128)S(1)}, s32[16]{0:T(128)}, u32[]{:S(2)}) copy-start(s32[16]{0:T(128)} %param.26) | copy-start | bytes 196
  98.1 12.4 %copy-start.3 = (s32[2,16]{1,0:T(2,128)S(1)}, s32[2,16]{1,0:T(2,128)}, u32[]{:S(2)}) copy-start(s32[2,16]{1,0:T(2,128)} %param.27) | copy-start | bytes 388
  98.1 28.0 %copy-start.6 = (s32[2]{0:T(128)S(1)}, s32[2]{0:T(128)}, u32[]{:S(2)}) copy-start(s32[2]{0:T(128)} %param.25) | copy-start | bytes 28
  98.1 84.1 %copy-start.2 = (bf16[2,256,3,128]{3,1,2,0:T(8,128)(2,1)S(1)}, bf16[2,256,3,128]{3,1,2,0:T(8,128)(2,1)}, u32[]{:S(2)}) copy-start(bf16[2,256,3,128]{3,1,2,0:T(8,128)(2,1)} %param.23) | copy-start | bytes 1179652
  98.1 85.2 %copy-start.5 = (bf16[2,256,3,128]{3,1,2,0:T(8,128)(2,1)S(1)}, bf16[2,256,3,128]{3,1,2,0:T(8,128)(2,1)}, u32[]{:S(2)}) copy-start(bf16[2,256,3,128]{3,1,2,0:T(8,128)(2,1)} %param.24) | copy-start | bytes 1179652
  98.1 47.7 %reduce-scatter.17.cloned.1.call-start = ((), (), s32[]{:S(2)}) async-start(), calls=%async_computation.18 | async-start | bytes 147456 | tf_op jit(solution)/shard_map/reduce_scatter | solution.py:60
  120.4 12.3 %all-to-all-start.2 = ((bf16[1,16,1,48]{3,2,0,1:T(2,128)(2,1)}), bf16[1,16,1,48]{3,2,0,1:T(2,128)(2,1)S(1)}, u32[]{:S(2)}, u32[]{:S(2)}) async-start(bf16[1,16,1,48]{3,2,0,1:T(2,128)(2,1)} %copy.114), calls=%async_computation.5 | async-start | bytes 16384 | tf_op jit(solution)/shard_map/all_to_all | solution.py:70
  132.6 9.8 %all-to-all-start.4 = ((bf16[1,16,1,48]{3,2,0,1:T(2,128)(2,1)}), bf16[1,16,1,48]{3,2,0,1:T(2,128)(2,1)S(1)}, u32[]{:S(2)}, u32[]{:S(2)}) async-start(bf16[1,16,1,48]{3,2,0,1:T(2,128)(2,1)} %copy.122), calls=%async_computation.10 | async-start | bytes 16384 | tf_op jit(solution)/shard_map/all_to_all | solution.py:69
  142.4 9.8 %all-to-all-start.1 = ((bf16[1,16,1,48]{3,2,0,1:T(2,128)(2,1)}), bf16[1,16,1,48]{3,2,0,1:T(2,128)(2,1)S(1)}, u32[]{:S(2)}, u32[]{:S(2)}) async-start(bf16[1,16,1,48]{3,2,0,1:T(2,128)(2,1)} %copy.112), calls=%async_computation.3 | async-start | bytes 16384 | tf_op jit(solution)/shard_map/all_to_all | solution.py:69
  152.2 9.8 %all-to-all-start.5 = ((bf16[1,16,1,48]{3,2,0,1:T(2,128)(2,1)}), bf16[1,16,1,48]{3,2,0,1:T(2,128)(2,1)S(1)}, u32[]{:S(2)}, u32[]{:S(2)}) async-start(bf16[1,16,1,48]{3,2,0,1:T(2,128)(2,1)} %copy.128), calls=%async_computation.12 | async-start | bytes 16384 | tf_op jit(solution)/shard_map/all_to_all | solution.py:70
  162.0 9.9 %all-to-all-start.3 = ((bf16[8,2,768]{2,1,0:T(2,128)(2,1)}), bf16[8,2,768]{2,1,0:T(2,128)(2,1)S(1)}, u32[]{:S(2)}, u32[]{:S(2)}) async-start(bf16[8,2,768]{2,1,0:T(2,128)(2,1)} %reshape.349), calls=%async_computation.8 | async-start | bytes 49152 | tf_op jit(solution)/shard_map/all_to_all | solution.py:68
  171.9 9.9 %all-to-all-start = ((bf16[8,2,768]{2,1,0:T(2,128)(2,1)}), bf16[8,2,768]{2,1,0:T(2,128)(2,1)S(1)}, u32[]{:S(2)}, u32[]{:S(2)}) async-start(bf16[8,2,768]{2,1,0:T(2,128)(2,1)} %reshape.351), calls=%async_computation.1 | async-start | bytes 49152 | tf_op jit(solution)/shard_map/all_to_all | solution.py:68
  175.2 95.6 %reduce-scatter.23.cloned.1.call-start = ((), (), s32[]{:S(2)}) async-start(), calls=%async_computation.21 | async-start | bytes 196608 | tf_op jit(solution)/shard_map/reduce_scatter | solution.py:121
  227.0 48.6 %reduce-scatter.15.cloned.1.call-start = ((), (), s32[]{:S(2)}) async-start(), calls=%async_computation.17 | async-start | bytes 196608 | tf_op jit(solution)/shard_map/reduce_scatter | solution.py:121
Sparse Core Ops, SparseCore 0:
  77.6 8.5 reduce-scatter.12
  88.4 8.5 reduce-scatter.18
  99.2 8.5 reduce-scatter.20
  109.8 8.5 reduce-scatter.10
  120.5 8.6 reduce-scatter.8
  131.2 8.6 reduce-scatter.16
  227.1 4.7 reduce-scatter.22
  270.9 4.6 reduce-scatter.14
where the time goes:
time: 285 us; the launch traced here: 284 us
  blocking collectives  129 us (45%)
  matrix products  60.7 us (21%)
  waiting for transfers between devices  36.2 us (13%)
  starting transfers between devices  22.9 us (8%)
  between operations  14 us (5%)
  local copies, waits for them, and re-layouts  13.1 us (5%)
  other arithmetic  8.4 us (3%)
    all_gather x2, blocking collectives, on_device(): gathered = lax.all_gather(block, 'row', axis=1, tiled=True)  64.3 us
    all_gather x2, blocking collectives, on_device(): lax.all_gather(attended_all, 'row', axis=1, tiled=True)  62.1 us
    dot_general x2, matrix products, on_device(): jnp.einsum('srd,hcd->srhc', normed, w_query[0], preferred_element_type=jn...  24.4 us
    dot_general x2, matrix products, on_device(): jnp.einsum('srf,hcf->srhc', lax.all_gather(attended_all, 'row', axis=1, t...  24.3 us
    all_to_all x2, waiting for transfers between devices, on_device(): lax.all_to_all(query_sorted, 'row', split_axis=1, concat_axis=3, tiled=True)  10.6 us
    all_to_all x2, waiting for transfers between devices, on_device(): lax.all_to_all(key_sorted, 'row', split_axis=1, concat_axis=3, tiled=True)  10 us
    all_to_all x2, starting transfers between devices, on_device(): lax.all_to_all(value_sorted, 'row', split_axis=1, concat_axis=3, tiled=True)  9.05 us
    all_to_all x2, waiting for transfers between devices, on_device(): lax.all_to_all(value_sorted, 'row', split_axis=1, concat_axis=3, tiled=True)  8.91 us
  transfers between devices with their start and end apart: 14, of which 8 were waited for; matrix products, arithmetic and copies ran while one was open for 22% of the time, Pallas kernels for 0%

commit v1 on v0

--- a/solution.py
+++ b/solution.py
@@ -1,6 +1,10 @@
+import functools
+
 import jax
 import jax.numpy as jnp
 from jax import lax
+from jax.experimental import pallas as pl
+from jax.experimental.pallas import tpu as pltpu
 from jax.sharding import PartitionSpec as P
 
 LAYER_AT = 63
@@ -127,9 +131,487 @@
     return jnp.concatenate(results, axis=0)
 
 
+MESH = pl.DeviceIdType.MESH
+LANES = 128
+Q_CHUNKS = 4
+NEG = float("-inf")
+
+
+def nt_dot(a, b):
+    return lax.dot_general(a, b, (((1,), (1,)), ((), ())), preferred_element_type=jnp.float32)
+
+
+def nn_dot(a, b):
+    return lax.dot_general(a, b, (((1,), (0,)), ((), ())), preferred_element_type=jnp.float32)
+
+
+def fused_kernel(
+    states,
+    gain,
+    w_query,
+    w_key,
+    w_value,
+    w_out,
+    key_cache,
+    value_cache,
+    cache_len,
+    slot_row,
+    exit_layer,
+    out,
+    gath,
+    wq,
+    wkv,
+    wo,
+    kc,
+    vc,
+    kext,
+    vext,
+    sums_own,
+    sums_in,
+    sums_all,
+    norm32,
+    normed,
+    acc,
+    acc_in,
+    a2a_out,
+    a2a_in,
+    q32,
+    ag,
+    att,
+    acc2,
+    acc2_in,
+    resid,
+    perm_q,
+    perm_a,
+    spread,
+    mask,
+    own_sem,
+    wq_sem,
+    wo_sem,
+    cache_sem,
+    gs_sem,
+    gr_sem,
+    ss_sem,
+    sr_sem,
+    rs_sem,
+    rr_sem,
+    as_sem,
+    ar_sem,
+    hs_sem,
+    hr_sem,
+):
+    me = lax.axis_index("row")
+    col = lax.axis_index("col")
+    other = 1 - col
+    x = lax.rem(me, 2)
+    z = lax.div(me, 2)
+    beside = me + 1 - 2 * x
+    along = [lax.rem(z + d, 4) * 2 + x for d in (1, 2, 3)]
+    across = [lax.rem(z + d, 4) * 2 + 1 - x for d in (0, 1, 2, 3)]
+    peers = [lax.rem(me + d, 8) for d in range(1, 8)]
+    half_width = gath.shape[2]
+    model_width = half_width * 2
+    k_chunk = half_width // Q_CHUNKS
+    q_width = wq.shape[1]
+    kv_width = w_key.shape[2]
+    out_width = wo.shape[1]
+    kv_heads = kext.shape[0]
+    slots = kc.shape[1]
+    o_chunk = wo.shape[2] // kv_heads
+    f32 = jnp.float32
+    bf16 = jnp.bfloat16
+
+    own = pltpu.make_async_copy(states, gath.at[me], own_sem)
+    own.start()
+    w_copies = []
+    for c in range(Q_CHUNKS):
+        cols = pl.ds(c * k_chunk, k_chunk)
+        group = []
+        for o in range(2):
+            group.append((w_query.at[0, o, :, cols], wq.at[o, :, cols]))
+            group.append((w_key.at[0, o, :, cols], wkv.at[pl.ds(o * LANES, kv_width), cols]))
+            group.append(
+                (w_value.at[0, o, :, cols], wkv.at[pl.ds(o * LANES + kv_width, kv_width), cols])
+            )
+        w_copies.append(
+            [
+                pltpu.make_async_copy(src, dst, wq_sem.at[c, i])
+                for i, (src, dst) in enumerate(group)
+            ]
+        )
+    o_copies = []
+    for g in range(kv_heads):
+        cols = pl.ds(g * o_chunk, o_chunk)
+        o_copies.append(
+            [
+                pltpu.make_async_copy(w_out.at[0, o, :, cols], wo.at[o, :, cols], wo_sem.at[g, o])
+                for o in range(2)
+            ]
+        )
+    c_copies = [
+        pltpu.make_async_copy(key_cache, kc, cache_sem.at[0]),
+        pltpu.make_async_copy(value_cache, vc, cache_sem.at[1]),
+    ]
+    for copy in w_copies[0] + c_copies:
+        copy.start()
+    for group in w_copies[1:] + o_copies:
+        for copy in group:
+            copy.start()
+
+    barrier = pltpu.get_barrier_semaphore()
+    for peer in peers:
+        pl.semaphore_signal(barrier, inc=1, device_id={"row": peer}, device_id_type=MESH)
+    pl.semaphore_signal(barrier, inc=1, device_id={"col": other}, device_id_type=MESH)
+    pl.semaphore_wait(barrier, 8)
+
+    sends = []
+
+    def push(src, dst, send_sem, recv_sem, where):
+        copy = pltpu.make_async_remote_copy(
+            src_ref=src,
+            dst_ref=dst,
+            send_sem=send_sem,
+            recv_sem=recv_sem,
+            device_id=where,
+            device_id_type=MESH,
+        )
+        copy.start()
+        sends.append(copy)
+
+    def landed(ref, recv_sem):
+        pltpu.make_async_remote_copy(
+            src_ref=ref,
+            dst_ref=ref,
+            send_sem=own_sem,
+            recv_sem=recv_sem,
+            device_id={"row": beside},
+            device_id_type=MESH,
+        ).wait_recv()
+
+    def spread_own(view, c, send_sem, recv_sem):
+        push(view(me), view(me), send_sem.at[c, 0], recv_sem.at[c, me], {"row": beside})
+        for i, peer in enumerate(along):
+            push(view(me), view(me), send_sem.at[c, 1 + i], recv_sem.at[c, me], {"row": peer})
+
+    def forward(view, c, send_sem, recv_sem):
+        for i, peer in enumerate(along):
+            landed(view(peer), recv_sem.at[c, peer])
+            push(view(peer), view(peer), send_sem.at[c, 4 + i], recv_sem.at[c, peer], {"row": beside})
+
+    def collect(view, c, recv_sem):
+        for peer in across:
+            landed(view(peer), recv_sem.at[c, peer])
+
+    def state_view(c):
+        return lambda peer: gath.at[peer, :, pl.ds(c * k_chunk, k_chunk)]
+
+    own.wait()
+    for c in range(Q_CHUNKS):
+        spread_own(state_view(c), c, gs_sem, gr_sem)
+
+    mine = gath[me].astype(f32)
+    square = jnp.sum(mine * mine, axis=1, keepdims=True)
+    sums_own[0:4, :] = jnp.broadcast_to(square, (4, LANES))
+    sums_own[4:8, :] = jnp.zeros((4, LANES), f32)
+    push(sums_own, sums_in, ss_sem.at[0], sr_sem.at[8], {"col": other})
+    landed(sums_in, sr_sem.at[8])
+    sums_all[me] = sums_own[...] + sums_in[...]
+    for i, peer in enumerate(peers):
+        push(sums_all.at[me], sums_all.at[me], ss_sem.at[1 + i], sr_sem.at[me], {"row": peer})
+
+    for o in range(2):
+        wkv[pl.ds(o * LANES + 2 * kv_width, LANES - 2 * kv_width), :] = jnp.zeros(
+            (LANES - 2 * kv_width, half_width), bf16
+        )
+    r = lax.broadcasted_iota(jnp.int32, (256, 1), 0)
+    slot_of = (r >> 5) * 2 + (r & 1)
+    target = jnp.zeros((256, 1), jnp.int32)
+    for t in range(16):
+        target = jnp.where(slot_of == t, slot_row[t], target)
+    q = lax.broadcasted_iota(jnp.int32, (256, 256), 1)
+    row_of = ((q >> 2) & 7) * 2 + (q & 1)
+    hit = (((r >> 2) & 7) == (q >> 5)) & (((r >> 1) & 1) == ((q >> 1) & 1)) & (row_of == target)
+    perm_q[...] = jnp.where(hit, 1.0, 0.0).astype(bf16)
+    q = lax.broadcasted_iota(jnp.int32, (1, 256), 1)
+    slot_of = (q >> 5) * 2 + (q & 1)
+    target = jnp.zeros((1, 256), jnp.int32)
+    for t in range(16):
+        target = jnp.where(slot_of == t, slot_row[t], target)
+    r = lax.broadcasted_iota(jnp.int32, (256, 256), 0)
+    hit = (((q >> 2) & 7) == (r >> 5)) & (((q >> 1) & 1) == ((r >> 4) & 1)) & ((r & 15) == target)
+    perm_a[...] = jnp.where(hit, 1.0, 0.0).astype(bf16)
+    n = lax.broadcasted_iota(jnp.int32, (LANES, 6 * LANES), 1)
+    lane = lax.broadcasted_iota(jnp.int32, (LANES, 6 * LANES), 0)
+    place = jnp.where(lane < kv_width, lane, lane - kv_width + 3 * LANES)
+    place = jnp.where(lane < 2 * kv_width, place, -10000)
+    for p in range(8):
+        spread[p * LANES : (p + 1) * LANES, :] = jnp.where(
+            n == place + p * kv_width, 1.0, 0.0
+        ).astype(bf16)
+    r = lax.broadcasted_iota(jnp.int32, mask.shape, 0)
+    k = lax.broadcasted_iota(jnp.int32, mask.shape, 1)
+    b = r & 1
+    s = (r >> 1) & 1
+    f = k - 2 * slots - 8
+    limit = b * slots + jnp.where(b == 0, cache_len[0], cache_len[1])
+    cached = (k >= b * slots) & (k < limit)
+    fresh = (f >= 0) & (f < 4) & ((f & 1) == b) & ((f >> 1) <= s)
+    mask[...] = jnp.where(cached | fresh, 0.0, NEG)
+    r = lax.broadcasted_iota(jnp.int32, (64, LANES), 0) & 3
+    exits = jnp.zeros((64, LANES), jnp.int32)
+    for step in range(2):
+        for slot in range(2):
+            layer = exit_layer[step, slot_row[me * 2 + slot]]
+            exits = jnp.where(r == step * 2 + slot, layer, exits)
+
+    def stage_caches():
+        for copy in c_copies:
+            copy.wait()
+        for slot in range(2):
+            for g in range(kv_heads):
+                kext[g, slot * slots : (slot + 1) * slots, :] = kc[slot, :, g, :]
+                vext[g, slot * slots : (slot + 1) * slots, :] = vc[slot, :, g, :]
+        for g in range(kv_heads):
+            kext[g, 2 * slots :, :] = jnp.zeros((LANES, LANES), bf16)
+            vext[g, 2 * slots :, :] = jnp.zeros((LANES, LANES), bf16)
+
+    forward(state_view(0), 0, gs_sem, gr_sem)
+    stage_caches()
+    for peer in peers:
+        landed(sums_all.at[peer], sr_sem.at[peer])
+    scale = [
+        lax.rsqrt(sums_all[p, 0:4, 0:1] / model_width + epsilon) for p in range(8)
+    ]
+    for c in range(Q_CHUNKS):
+        cols = pl.ds(c * k_chunk, k_chunk)
+        if c + 1 < Q_CHUNKS:
+            forward(state_view(c + 1), c + 1, gs_sem, gr_sem)
+        collect(state_view(c), c, gr_sem)
+        for p in range(8):
+            norm32[p * 4 : (p + 1) * 4, :] = (
+                gath[p, :, cols].astype(f32) * scale[p] * gain[:, cols]
+            )
+        normed[...] = norm32[...].astype(bf16)
+        for copy in w_copies[c]:
+            copy.wait()
+
+        kv = nt_dot(normed[...], wkv[:, cols])
+        for o in range(2):
+            part = kv[:, o * LANES : (o + 1) * LANES]
+            if c == 0:
+                acc[o, :, q_width:] = part
+            else:
+                acc[o, :, q_width:] += part
+
+        def query_tiles(half, c=c, cols=cols):
+            @pl.loop(0, q_width // 256)
+            def _(i):
+                at = pl.ds(pl.multiple_of(i * 256, 256), 256)
+                part = nt_dot(normed[...], wq[half, at, cols])
+                if c == 0:
+                    acc[half, :, at] = part
+                else:
+                    acc[half, :, at] += part
+
+        query_tiles(other)
+        if c == Q_CHUNKS - 1:
+            push(acc.at[other], acc_in, rs_sem.at[0], rr_sem.at[0], {"col": other})
+        query_tiles(col)
+
+    for p in range(8):
+        piece = gath[p, :, pl.ds(pl.multiple_of(me * out_width, out_width), out_width)].astype(f32)
+        for step in range(2):
+            resid[step * 16 + p * 2 : step * 16 + p * 2 + 2, :] = piece[step * 2 : step * 2 + 2]
+
+    landed(acc_in, rr_sem.at[0])
+    total = (acc[col] + acc_in[...]).astype(bf16)
+    stack = [total[:, j * LANES : (j + 1) * LANES] for j in range(7)]
+    stack.append(jnp.zeros((32, LANES), bf16))
+    a2a_out[...] = nn_dot(perm_q[...], jnp.concatenate(stack, axis=0)).astype(bf16)
+    for i, peer in enumerate(peers):
+        push(
+            a2a_out.at[pl.ds(pl.multiple_of(peer * 32, 32), 32), :],
+            a2a_in.at[me],
+            as_sem.at[i],
+            ar_sem.at[me],
+            {"row": peer},
+        )
+    a2a_in[me] = a2a_out[pl.ds(pl.multiple_of(me * 32, 32), 32), :]
+    for peer in peers:
+        landed(a2a_in.at[peer], ar_sem.at[peer])
+
+    news = jnp.concatenate([a2a_in[p, 16:32, :] for p in range(8)], axis=1)
+    news = nn_dot(news, spread[...]).astype(bf16)
+    for g in range(kv_heads):
+        kext[g, 2 * slots : 2 * slots + 16, :] = news[:, g * LANES : (g + 1) * LANES]
+        vext[g, 2 * slots : 2 * slots + 16, :] = news[
+            :, (kv_heads + g) * LANES : (kv_heads + g + 1) * LANES
+        ]
+    for p in range(8):
+        q32[p * 24 : (p + 1) * 24, :] = a2a_in[p].astype(f32)[0:24]
+
+    def heads_view(g):
+        return lambda peer: ag.at[peer, pl.ds(g * 64, 64), :]
+
+    for g in range(kv_heads):
+        scores = nt_dot(q32[g * 64 : (g + 1) * 64, :].astype(bf16), kext[g]) * (LANES ** -0.5)
+        scores = scores + mask[...]
+        exps = jnp.exp(scores - jnp.max(scores, axis=1, keepdims=True))
+        probs = (exps / jnp.sum(exps, axis=1, keepdims=True)).astype(bf16)
+        result = nn_dot(probs, vext[g])
+        result = jnp.where(exits > LAYER_AT, result, 0.0)
+        ag[me, g * 64 : (g + 1) * 64, :] = result.astype(bf16)
+        spread_own(heads_view(g), g, hs_sem, hr_sem)
+
+    forward(heads_view(0), 0, hs_sem, hr_sem)
+    for g in range(kv_heads):
+        if g + 1 < kv_heads:
+            forward(heads_view(g + 1), g + 1, hs_sem, hr_sem)
+        collect(heads_view(g), g, hr_sem)
+        for block in range(2):
+            at = g * 64 + block * 32
+            rows = ag[:, at : at + 32, :].reshape(256, LANES)
+            tiles = nn_dot(perm_a[...], rows).astype(bf16)
+            for j in range(8):
+                lanes = (block * 8 + j) * LANES
+                att[:, lanes : lanes + LANES] = tiles[j * 32 : (j + 1) * 32, :]
+        for copy in o_copies[g]:
+            copy.wait()
+
+        def out_tiles(half, g=g):
+            @pl.loop(0, out_width // 256)
+            def _(i):
+                at = pl.ds(pl.multiple_of(i * 256, 256), 256)
+                part = nt_dot(att[...], wo[half, at, pl.ds(g * o_chunk, o_chunk)])
+                if g == 0:
+                    acc2[half, :, at] = part
+                else:
+                    acc2[half, :, at] += part
+
+        out_tiles(other)
+        if g == kv_heads - 1:
+            push(acc2.at[other], acc2_in, rs_sem.at[1], rr_sem.at[1], {"col": other})
+        out_tiles(col)
+    resid[...] += acc2[col]
+    landed(acc2_in, rr_sem.at[1])
+    final = (resid[...] + acc2_in[...]).astype(bf16)
+    for step in range(2):
+        out[step] = final[step * 16 : (step + 1) * 16, :]
+    for copy in sends:
+        copy.wait_send()
+
+
+def fused(
+    states,
+    norm_gain,
+    w_query,
+    w_key,
+    w_value,
+    w_out,
+    key_cache,
+    value_cache,
+    cache_len,
+    slot_row,
+    exit_layer,
+):
+    steps, own_rows, _, half_width = states.shape
+    kv_heads = key_cache.shape[2]
+    slots = key_cache.shape[1]
+    q_width = w_query.shape[2]
+    out_width = w_out.shape[2]
+    head_width = w_out.shape[3]
+    any_space = pl.BlockSpec(memory_space=pl.ANY)
+    vmem = pl.BlockSpec(memory_space=pltpu.VMEM)
+    smem = pl.BlockSpec(memory_space=pltpu.SMEM)
+    f32 = jnp.float32
+    bf16 = jnp.bfloat16
+    keys = 2 * slots + LANES
+    dma = pltpu.SemaphoreType.DMA
+    result = pl.pallas_call(
+        fused_kernel,
+        out_shape=jax.ShapeDtypeStruct((steps, 16, out_width), bf16),
+        in_specs=[any_space, vmem] + [any_space] * 6 + [smem] * 3,
+        out_specs=vmem,
+        scratch_shapes=[
+            pltpu.VMEM((8, steps * own_rows, half_width), bf16),
+            pltpu.VMEM((2, q_width, half_width), bf16),
+            pltpu.VMEM((2 * LANES, half_width), bf16),
+            pltpu.VMEM((2, out_width, head_width), bf16),
+            pltpu.VMEM(key_cache.shape, bf16),
+            pltpu.VMEM(value_cache.shape, bf16),
+            pltpu.VMEM((kv_heads, keys, LANES), bf16),
+            pltpu.VMEM((kv_heads, keys, LANES), bf16),
+            pltpu.VMEM((8, LANES), f32),
+            pltpu.VMEM((8, LANES), f32),
+            pltpu.VMEM((8, 8, LANES), f32),
+            pltpu.VMEM((32, half_width // Q_CHUNKS), f32),
+            pltpu.VMEM((32, half_width // Q_CHUNKS), bf16),
+            pltpu.VMEM((2, 32, q_width + LANES), f32),
+            pltpu.VMEM((32, q_width + LANES), f32),
+            pltpu.VMEM((256, LANES), bf16),
+            pltpu.VMEM((8, 32, LANES), bf16),
+            pltpu.VMEM((192, LANES), f32),
+            pltpu.VMEM((8, 192, LANES), bf16),
+            pltpu.VMEM((32, head_width // kv_heads), bf16),
+            pltpu.VMEM((2, 32, out_width), f32),
+            pltpu.VMEM((32, out_width), f32),
+            pltpu.VMEM((32, out_width), f32),
+            pltpu.VMEM((256, 256), bf16),
+            pltpu.VMEM((256, 256), bf16),
+            pltpu.VMEM((8 * LANES, 6 * LANES), bf16),
+            pltpu.VMEM((64, keys), f32),
+            dma,
+            dma((Q_CHUNKS, 6)),
+            dma((kv_heads, 2)),
+            dma((2,)),
+            dma((Q_CHUNKS, 7)),
+            dma((Q_CHUNKS, 8)),
+            dma((8,)),
+            dma((9,)),
+            dma((2,)),
+            dma((2,)),
+            dma((7,)),
+            dma((8,)),
+            dma((kv_heads, 7)),
+            dma((kv_heads, 8)),
+        ],
+        compiler_params=pltpu.CompilerParams(
+            collective_id=0, has_side_effects=True, vmem_limit_bytes=63 * 1024 * 1024
+        ),
+        name="fused_layer",
+    )(
+        states.reshape(steps * own_rows, half_width),
+        norm_gain,
+        w_query,
+        w_key,
+        w_value,
+        w_out,
+        key_cache,
+        value_cache,
+        cache_len,
+        slot_row,
+        exit_layer,
+    )
+    return result[:, :, None, :]
+
+
+def on_device_any(*args):
+    states, _, w_query, w_key, _, w_out, key_cache = args[:7]
+    fits = (
+        lax.axis_size("row") == 8
+        and lax.axis_size("col") == 2
+        and states.shape[:2] == (2, 2)
+        and w_query.shape[1:3] == (2, 6 * LANES)
+        and w_key.shape[2] == 48
+        and key_cache.shape[2:] == (3, LANES)
+        and w_out.shape[3] == 48 * LANES
+    )
+    return fused(*args) if fits else on_device(*args)
+
+
 def solution(mesh):
     return jax.shard_map(
-        on_device,
+        on_device_any,
         mesh=mesh,
         in_specs=(
             P(None, ("groups", "row"), "col", None),

time: 285 us -> 73.2 us (0.26)
  blocking collectives: 129 us -> 0 us
  Pallas kernels: 0 us -> 65.6 us
  matrix products: 60.7 us -> 0 us
  waiting for transfers between devices: 36.2 us -> 0 us
  starting transfers between devices: 22.9 us -> 0 us
  between operations: 14 us -> 0.01 us
  other arithmetic: 8.4 us -> 0 us
  local copies, waits for them, and re-layouts: 13.1 us -> 7.24 us
    all_gather x4 -> x0, blocking collectives: 126 us -> none  [the longest x2 64.3 us: on_device(): gathered = lax.all_gather(block, 'row', axis=1, tiled=True)]
    pallas_call x0 -> x1, Pallas kernels: none -> 65.6 us  [fused(): pl.pallas_call(fused_kernel, out_shape=jax.ShapeDtypeStruct((steps, 16, o...]
    dot_general x16 -> x0, matrix products: 60.7 us -> none  [the longest x2 24.4 us: on_device(): jnp.einsum('srd,hcd->srhc', normed, w_query[0], preferred_element_type=jn...]
    all_to_all x6 -> x0, waiting for transfers between devices: 29.6 us -> none  [the longest x2 10.6 us: on_device(): lax.all_to_all(query_sorted, 'row', split_axis=1, concat_axis=3, tiled=True)]
    all_to_all x6 -> x0, starting transfers between devices: 22.4 us -> none  [the longest x2 9.05 us: on_device(): lax.all_to_all(value_sorted, 'row', split_axis=1, concat_axis=3, tiled=True)]
    reduce_scatter x8 -> x0, waiting for transfers between devices: 6.45 us -> none  [the longest x2 3.77 us: on_device(): lax.psum_scatter(projection_terms, 'col', scatter_dimension=2, tiled=True)]
    gather x8 -> x0, local copies, waits for them, and re-layouts: 4.75 us -> none  [the longest x2 1.28 us: on_device(): active = jnp.take(exit_layer[first_step], own_slots) > LAYER_AT]
    another operation x8 -> x0, other arithmetic: 4.43 us -> none  [the longest x2 1.61 us: on_device(): query_sorted = jnp.take(query_sum.astype(jnp.bfloat16), slot_row, axis=1)]
  transfers between devices with their start and end apart: 14 -> 0, of which waited for: 8 -> 0; matrix products, arithmetic and copies ran while one was open for 22% -> 0% of each run, Pallas kernels for 0% -> 0%
where the time goes in v1:
time: 73.2 us; the launch traced here: 72.9 us
  Pallas kernels  65.6 us (90%)
  local copies, waits for them, and re-layouts  7.24 us (10%)
    pallas_call x1, Pallas kernels, fused(): pl.pallas_call(fused_kernel, out_shape=jax.ShapeDtypeStruct((steps, 16, o...  65.6 us
    unnamed x3, local copies, waits for them, and re-layouts  5.74 us
    reshape x1, local copies, waits for them, and re-layouts, fused(): states.reshape(steps * own_rows, half_width)  1.5 us

profile of v1, /device:TPU:0, one launch (start us, length us, event | category | flops | bytes accessed | tf_op | source)
XLA Modules:
  0.0 72.9 jit_solution(9566119705993387882)
XLA Ops:
  0.0 1.5 %reshape.3.states = bf16[4,8192]{1,0:T(4,128)(2,1)} reshape(bf16[2,2,1,8192]{3,1,2,0:T(2,128)(2,1)} %param.11) | data formatting | bytes 131072 | tf_op jit(solution)/shard_map/reshape | solution.py:583
  1.5 2.1 %copy.12.key_cache = bf16[2,256,3,128]{3,2,1,0:T(4,128)(2,1)} copy(bf16[2,256,3,128]{3,1,2,0:T(8,128)(2,1)} %param.17) | data formatting | bytes 786432 | tf_op args[6]
  3.6 2.1 %copy.13.value_cache = bf16[2,256,3,128]{3,2,1,0:T(4,128)(2,1)} copy(bf16[2,256,3,128]{3,1,2,0:T(8,128)(2,1)} %param.18) | data formatting | bytes 786432 | tf_op args[7]
  5.8 65.6 %fused_layer.1 = bf16[2,16,1024]{2,1,0:T(8,128)(2,1)} custom-call(bf16[4,8192]{1,0:T(4,128)(2,1)} %reshape.3.states, f32[1,8192]{1,0:T(1,128)} %gain.1, bf16[1,2,768,8192]{3,2,1,0:T(8,128)(2,1)} %w_query.1, bf16[1,2,48,8192]{3,2,1,0:T(8,128)(2,1)} %w_key.1, bf16[1,2,48,8192]{3,2,1,0:T(8,128)(2,1)} %w_value.1, bf16[1,2,1024,6144]{3,2,1,0:T(8,128)(2,1)} %w_out.1, ...), custom_call_target="tpu_custom_call" | custom-call | tf_op jit(solution)/shard_map/fused_layer/pallas_call | solution.py:530
  71.4 1.5 %copy.16 = bf16[2,16,1,1024]{3,1,2,0:T(8,128)(2,1)} copy(bf16[2,16,1,1024]{3,1,2,0:T(8,128)(2,1)} %bitcast.5) | data formatting | bytes 131072

commit v2 on v1

--- a/solution.py
+++ b/solution.py
@@ -169,6 +169,8 @@
     sums_own,
     sums_in,
     sums_all,
+    own_rows,
+    own32,
     norm32,
     normed,
     acc,
@@ -216,12 +218,12 @@
     kv_width = w_key.shape[2]
     out_width = wo.shape[1]
     kv_heads = kext.shape[0]
-    slots = kc.shape[1]
+    slots = kc.shape[2]
     o_chunk = wo.shape[2] // kv_heads
     f32 = jnp.float32
     bf16 = jnp.bfloat16
 
-    own = pltpu.make_async_copy(states, gath.at[me], own_sem)
+    own = pltpu.make_async_copy(states, own_rows, own_sem)
     own.start()
     w_copies = []
     for c in range(Q_CHUNKS):
@@ -306,10 +308,13 @@
         return lambda peer: gath.at[peer, :, pl.ds(c * k_chunk, k_chunk)]
 
     own.wait()
+    for step in range(2):
+        own32[step * 2 : step * 2 + 2, :] = own_rows[step].astype(f32)
+    gath[me] = own32[...].astype(bf16)
     for c in range(Q_CHUNKS):
         spread_own(state_view(c), c, gs_sem, gr_sem)
 
-    mine = gath[me].astype(f32)
+    mine = own32[...]
     square = jnp.sum(mine * mine, axis=1, keepdims=True)
     sums_own[0:4, :] = jnp.broadcast_to(square, (4, LANES))
     sums_own[4:8, :] = jnp.zeros((4, LANES), f32)
@@ -369,8 +374,8 @@
             copy.wait()
         for slot in range(2):
             for g in range(kv_heads):
-                kext[g, slot * slots : (slot + 1) * slots, :] = kc[slot, :, g, :]
-                vext[g, slot * slots : (slot + 1) * slots, :] = vc[slot, :, g, :]
+                kext[g, slot * slots : (slot + 1) * slots, :] = kc[slot, g]
+                vext[g, slot * slots : (slot + 1) * slots, :] = vc[slot, g]
         for g in range(kv_heads):
             kext[g, 2 * slots :, :] = jnp.zeros((LANES, LANES), bf16)
             vext[g, 2 * slots :, :] = jnp.zeros((LANES, LANES), bf16)
@@ -537,13 +542,15 @@
             pltpu.VMEM((2, q_width, half_width), bf16),
             pltpu.VMEM((2 * LANES, half_width), bf16),
             pltpu.VMEM((2, out_width, head_width), bf16),
-            pltpu.VMEM(key_cache.shape, bf16),
-            pltpu.VMEM(value_cache.shape, bf16),
+            pltpu.VMEM((own_rows, kv_heads, slots, LANES), bf16),
+            pltpu.VMEM((own_rows, kv_heads, slots, LANES), bf16),
             pltpu.VMEM((kv_heads, keys, LANES), bf16),
             pltpu.VMEM((kv_heads, keys, LANES), bf16),
             pltpu.VMEM((8, LANES), f32),
             pltpu.VMEM((8, LANES), f32),
             pltpu.VMEM((8, 8, LANES), f32),
+            pltpu.VMEM((steps, own_rows, half_width), bf16),
+            pltpu.VMEM((steps * own_rows, half_width), f32),
             pltpu.VMEM((32, half_width // Q_CHUNKS), f32),
             pltpu.VMEM((32, half_width // Q_CHUNKS), bf16),
             pltpu.VMEM((2, 32, q_width + LANES), f32),
@@ -580,14 +587,14 @@
         ),
         name="fused_layer",
     )(
-        states.reshape(steps * own_rows, half_width),
+        states.transpose(0, 2, 1, 3)[:, 0],
         norm_gain,
         w_query,
         w_key,
         w_value,
         w_out,
-        key_cache,
-        value_cache,
+        key_cache.transpose(0, 2, 1, 3),
+        value_cache.transpose(0, 2, 1, 3),
         cache_len,
         slot_row,
         exit_layer,

time: 73.2 us -> 67 us (0.915)
  local copies, waits for them, and re-layouts: 7.24 us -> 1.47 us
    unnamed x3 -> x1, local copies, waits for them, and re-layouts: 5.74 us -> 1.47 us
    reshape x1 -> x0, local copies, waits for them, and re-layouts: 1.5 us -> none  [fused(): states.reshape(steps * own_rows, half_width)]
where the time goes in v2:
time: 67 us; the launch traced here: 66.7 us
  Pallas kernels  65.3 us (97%)
  local copies, waits for them, and re-layouts  1.47 us (2%)
    pallas_call x1, Pallas kernels, fused(): pl.pallas_call(fused_kernel, out_shape=jax.ShapeDtypeStruct((steps, 16, o...  65.3 us
    unnamed x1, local copies, waits for them, and re-layouts  1.47 us

profile of v2, /device:TPU:0, one launch (start us, length us, event | category | flops | bytes accessed | tf_op | source)
XLA Modules:
  0.0 66.7 jit_solution(5088232520016973746)
XLA Ops:
  0.0 65.3 %fused_layer.1 = bf16[2,16,1024]{2,1,0:T(8,128)(2,1)} custom-call(bf16[2,2,8192]{2,1,0:T(2,128)(2,1)} %bitcast.9, f32[1,8192]{1,0:T(1,128)} %gain.1, bf16[1,2,768,8192]{3,2,1,0:T(8,128)(2,1)} %w_query.1, bf16[1,2,48,8192]{3,2,1,0:T(8,128)(2,1)} %w_key.1, bf16[1,2,48,8192]{3,2,1,0:T(8,128)(2,1)} %w_value.1, bf16[1,2,1024,6144]{3,2,1,0:T(8,128)(2,1)} %w_out.1, ...), custom_call_target="tpu_custom_call" | custom-call | tf_op jit(solution)/shard_map/fused_layer/pallas_call | solution.py:535
  65.3 1.5 %copy.14 = bf16[2,16,1,1024]{3,1,2,0:T(8,128)(2,1)} copy(bf16[2,16,1,1024]{3,1,2,0:T(8,128)(2,1)} %bitcast.8) | data formatting | bytes 131072

commit v3 on v2

--- a/solution.py
+++ b/solution.py
@@ -255,10 +255,10 @@
         pltpu.make_async_copy(value_cache, vc, cache_sem.at[1]),
     ]
     for copy in w_copies[0] + c_copies:
-        copy.start()
-    for group in w_copies[1:] + o_copies:
+        copy.start(priority=1)
+    for group in w_copies[1:]:
         for copy in group:
-            copy.start()
+            copy.start(priority=1)
 
     barrier = pltpu.get_barrier_semaphore()
     for peer in peers:
@@ -392,6 +392,9 @@
         if c + 1 < Q_CHUNKS:
             forward(state_view(c + 1), c + 1, gs_sem, gr_sem)
         collect(state_view(c), c, gr_sem)
+        if c >= 1:
+            for copy in o_copies[c - 1]:
+                copy.start(priority=1)
         for p in range(8):
             norm32[p * 4 : (p + 1) * 4, :] = (
                 gath[p, :, cols].astype(f32) * scale[p] * gain[:, cols]
@@ -409,7 +412,7 @@
                 acc[o, :, q_width:] += part
 
         def query_tiles(half, c=c, cols=cols):
-            @pl.loop(0, q_width // 256)
+            @pl.loop(0, q_width // 256, unroll=True)
             def _(i):
                 at = pl.ds(pl.multiple_of(i * 256, 256), 256)
                 part = nt_dot(normed[...], wq[half, at, cols])
@@ -484,7 +487,7 @@
             copy.wait()
 
         def out_tiles(half, g=g):
-            @pl.loop(0, out_width // 256)
+            @pl.loop(0, out_width // 256, unroll=True)
             def _(i):
                 at = pl.ds(pl.multiple_of(i * 256, 256), 256)
                 part = nt_dot(att[...], wo[half, at, pl.ds(g * o_chunk, o_chunk)])

time: 67 us -> 51.2 us (0.76)
  Pallas kernels: 65.3 us -> 49.4 us
    pallas_call x1, Pallas kernels: 65.3 us -> 49.4 us  [fused(): pl.pallas_call(fused_kernel, out_shape=jax.ShapeDtypeStruct((steps, 16, o...]
where the time goes in v3:
time: 51.2 us; the launch traced here: 50.9 us
  Pallas kernels  49.4 us (96%)
  local copies, waits for them, and re-layouts  1.47 us (3%)
    pallas_call x1, Pallas kernels, fused(): pl.pallas_call(fused_kernel, out_shape=jax.ShapeDtypeStruct((steps, 16, o...  49.4 us
    unnamed x1, local copies, waits for them, and re-layouts  1.47 us

profile of v3, /device:TPU:0, one launch (start us, length us, event | category | flops | bytes accessed | tf_op | source)
XLA Modules:
  0.0 50.9 jit_solution(16324039375160230930)
XLA Ops:
  0.0 49.4 %fused_layer.1 = bf16[2,16,1024]{2,1,0:T(8,128)(2,1)} custom-call(bf16[2,2,8192]{2,1,0:T(2,128)(2,1)} %bitcast.9, f32[1,8192]{1,0:T(1,128)} %gain.1, bf16[1,2,768,8192]{3,2,1,0:T(8,128)(2,1)} %w_query.1, bf16[1,2,48,8192]{3,2,1,0:T(8,128)(2,1)} %w_key.1, bf16[1,2,48,8192]{3,2,1,0:T(8,128)(2,1)} %w_value.1, bf16[1,2,1024,6144]{3,2,1,0:T(8,128)(2,1)} %w_out.1, ...), custom_call_target="tpu_custom_call" | custom-call | tf_op jit(solution)/shard_map/fused_layer/pallas_call | solution.py:538
  49.5 1.5 %copy.14 = bf16[2,16,1,1024]{3,1,2,0:T(8,128)(2,1)} copy(bf16[2,16,1,1024]{3,1,2,0:T(8,128)(2,1)} %bitcast.8) | data formatting | bytes 131072
